TPU v7x, 32 devices: a whole 2x2x4 slice. The times are simulated.
32 devices in a mesh: tgt: 8 (over y, x, core), src: 4 (over z).
Axes of the slice: x: 2, y: 2, z: 4, core: 2. Of those that a mesh axis runs over, the one named last changes fastest.
Arguments:
- states_late: bfloat16 [8192, 128], P('src'), may hold values from -12 to 12
- offset_late: bfloat16 [8192], P('src'), may hold values from 0 to 2
- values_late: bfloat16 [8192, 64], P('src'), may hold values from -6 to 6
- states_mid: bfloat16 [8192, 128], P('tgt'), may hold values from -12 to 12
- offset_mid: bfloat16 [8192], P('src'), may hold values from 0 to 2
- exercise_mid: bfloat16 [8192, 64], P('tgt'), may hold values from -6 to 6
- mask_mid: int32 [16, 16], replicated, may hold values from 0 to 1, as said below
- states_early: bfloat16 [8192, 128], P('tgt'), may hold values from -12 to 12
- exercise_early: bfloat16 [8192, 64], P('tgt'), may hold values from -6 to 6
- mask_early: int32 [16, 16], replicated, may hold values from 0 to 1, as said below
Outputs:
- value_mid: bfloat16 [8192, 64], P('tgt')
- value_early: bfloat16 [8192, 64], P('tgt')
Inputs may be any that keep to these rules, and one draw needn't show every extreme that they name: `mask_mid`: 1 marks a live tile of 512 x 512 paths; every diagonal tile is live. `mask_early`: 1 marks a live tile of 512 x 512 paths; every diagonal tile is live.
All inputs are finite; a program needn't handle non-finite values.
Results may differ from a plain program's by a relative error of at most 0.0055.
Values may be sent and summed in bfloat16 or wider, within the bound.
A program may use at most 64 MiB of HBM per device.

v0:
```python
import jax
import jax.numpy as jnp
from jax import lax
from jax.sharding import PartitionSpec as P

BLOCK = 512


sharpness = 3.5
very_low = -1e30


def date_partials(targets, sources, offsets, values, tile_mask):
    row_count = targets.shape[0]
    col_count = sources.shape[0]
    factors = targets.shape[1]
    value_width = values.shape[1]
    row_tiles = row_count // BLOCK
    col_tiles = col_count // BLOCK
    score_scale = sharpness / factors**0.5
    local_mask = lax.dynamic_slice(
        tile_mask,
        (lax.axis_index("tgt") * row_tiles, lax.axis_index("src") * col_tiles),
        (row_tiles, col_tiles),
    )
    source_tiles = sources.reshape(col_tiles, BLOCK, factors)
    offset_tiles = offsets.astype(jnp.float32).reshape(col_tiles, BLOCK)
    value_tiles = values.reshape(col_tiles, BLOCK, value_width)
    peaks, sums, weighted_all = ([], [], [])
    for row_block in range(row_tiles):
        target_rows = targets[row_block * BLOCK : (row_block + 1) * BLOCK]

        def step(carry, inputs):
            source_tile, offset_tile, value_tile, tile_live = inputs

            def active(carry_in):
                row_peak, weight_sum, weighted = carry_in
                scores = lax.dot_general(
                    target_rows,
                    source_tile,
                    (((1,), (1,)), ((), ())),
                    preferred_element_type=jnp.float32,
                )
                scores = scores * score_scale - offset_tile[None, :]
                new_peak = jnp.maximum(row_peak, jnp.max(scores, axis=1))
                shrink = jnp.exp(row_peak - new_peak)
                weights = jnp.exp(scores - new_peak[:, None])
                new_sum = weight_sum * shrink + jnp.sum(weights, axis=1)
                new_weighted = weighted * shrink[:, None] + jnp.dot(
                    weights.astype(jnp.bfloat16), value_tile, preferred_element_type=jnp.float32
                )
                return (new_peak, new_sum, new_weighted)

            def skipped(carry_in):
                return carry_in

            return (lax.cond(tile_live > 0, active, skipped, carry), None)

        start = (
            jnp.full((BLOCK,), very_low, jnp.float32),
            jnp.zeros((BLOCK,), jnp.float32),
            jnp.zeros((BLOCK, value_width), jnp.float32),
        )
        result, _ = lax.scan(
            step, start, (source_tiles, offset_tiles, value_tiles, local_mask[row_block])
        )
        peaks.append(result[0])
        sums.append(result[1])
        weighted_all.append(result[2])
    return (jnp.concatenate(peaks, 0), jnp.concatenate(sums, 0), jnp.concatenate(weighted_all, 0))


def finish(partials, exercise):
    row_peak, weight_sum, weighted = partials
    peak_all = lax.pmax(row_peak, "src")
    shrink = jnp.exp(row_peak - peak_all)
    weight_sum, weighted = lax.psum((weight_sum * shrink, weighted * shrink[:, None]), "src")
    continuation = weighted / weight_sum[:, None]
    return jnp.maximum(continuation, exercise.astype(jnp.float32)).astype(jnp.bfloat16)


def regroup(block_rows):
    per_owner = lax.axis_size("tgt") // lax.axis_size("src")
    gathered = lax.all_gather(block_rows, "tgt", axis=0, tiled=True)
    row_count = block_rows.shape[0] * per_owner
    return lax.dynamic_slice_in_dim(gathered, lax.axis_index("src") * row_count, row_count, 0)


def per_device(
    states_late,
    offset_late,
    values_late,
    states_mid,
    offset_mid,
    exercise_mid,
    mask_mid,
    states_early,
    exercise_early,
    mask_early,
):
    mid_sources = regroup(states_mid)
    value_mid = finish(
        date_partials(states_mid, states_late, offset_late, values_late, mask_mid), exercise_mid
    )
    mid_values = regroup(value_mid)
    value_early = finish(
        date_partials(states_early, mid_sources, offset_mid, mid_values, mask_early), exercise_early
    )
    return (value_mid, value_early)


def solution(mesh):
    in_specs = (
        P("src", None),
        P("src"),
        P("src", None),
        P("tgt", None),
        P("src"),
        P("tgt", None),
        P(),
        P("tgt", None),
        P("tgt", None),
        P(),
    )
    out_specs = (P("tgt", None), P("tgt", None))
    return jax.shard_map(
        per_device, mesh=mesh, in_specs=in_specs, out_specs=out_specs, check_vma=False
    )
```

profile of v0, /device:TPU:0, one launch (start us, length us, event | category | flops | bytes accessed | tf_op | source)
XLA Modules:
  0.0 209.8 jit_solution(14722744577030055065)
XLA Ops:
  11.0 12.8 %while.57 = (s32[]{:T(128)}, f32[512]{0:T(512)S(1)}, f32[512]{0:T(512)S(1)}, f32[512,64]{0,1:T(8,128)S(1)}, s32[4]{0:T(128)S(1)}, /*index=5*/bf16[4,512,128]{2,1...) while((s32[]{:T(128)}, f32[512]{0:T(512)S(1)}, ...), condition=%wide.region_11.12_spmd, body=%wide.region_6.11_spmd.sunk | while | flops 102564864 | bytes 3840783 | solution.py:64
  12.3 1.8 conditional.9
  15.5 1.8 conditional.9
  18.8 1.8 conditional.9
  22.0 1.8 conditional.9
  23.9 12.0 %while.56 = (s32[]{:T(128)}, f32[512]{0:T(512)S(1)}, f32[512]{0:T(512)S(1)}, f32[512,64]{0,1:T(8,128)S(1)}, s32[4]{0:T(128)S(1)}, /*index=5*/bf16[4,512,128]{2,1...) while((s32[]{:T(128)}, f32[512]{0:T(512)S(1)}, ...), condition=%wide.region_5.6_spmd, body=%wide.region_0.5_spmd.sunk | while | flops 102564864 | bytes 3840783 | solution.py:64
  25.0 1.8 conditional.8
  25.1 1.2 fusion.44
  28.0 1.8 conditional.8
  28.1 1.2 fusion.44
  31.0 1.8 conditional.8
  34.0 1.8 conditional.8
  35.9 9.8 %pmax.14 = f32[1024]{0:T(1024)S(1)} all-reduce(f32[1024]{0:T(1024)S(1)} %constant_dynamic-update-slice_fusion), channel_id=1, replica_groups=mesh['tgt'=8,'src'=4] {'src'}, use_global_device_ids=true, to_apply=%region_12.13 | all-reduce | flops 1024 | bytes 8192 | tf_op jit(solution)/shard_map/pmax | solution.py:75
  46.5 9.0 %psum.29 = f32[1024]{0:T(1024)S(1)} all-reduce(f32[1024]{0:T(1024)S(1)} %get-tuple-element.638), channel_id=1, replica_groups=mesh['tgt'=8,'src'=4] {'src'}, use_global_device_ids=true, to_apply=%region_14.15 | all-reduce | flops 1024 | bytes 8192 | tf_op jit(solution)/shard_map/psum | solution.py:77
  55.5 28.3 %all-reduce.3.cloned.1.call-done = f32[1024,64]{0,1:T(8,128)} async-done(((f32[1024,64]{0,1:T(8,128)}), f32[1024,64]{0,1:T(8,128)}) %all-reduce.3.cloned.1.call-update) | async-done | bytes 262160 | tf_op jit(solution)/shard_map/psum | solution.py:77
  83.7 1.6 maximum_convert_fusion.1
  87.0 22.6 %all-gather.5.cloned.1.call-done = bf16[8192,64]{0,1:T(8,128)(2,1)} async-done(((bf16[1024,64]{0,1:T(8,128)(2,1)}), bf16[8192,64]{0,1:T(8,128)(2,1)}) %all-gather.5.cloned.1.call-update) | async-done | bytes 1048592 | tf_op jit(solution)/shard_map/all_gather | solution.py:84
  110.9 28.7 %all-gather.3.cloned.1.call-done = bf16[8192,128]{1,0:T(8,128)(2,1)} async-done(((bf16[1024,128]{1,0:T(8,128)(2,1)}), bf16[8192,128]{1,0:T(8,128)(2,1)}) %all-gather.3.cloned.1.call-update) | async-done | bytes 2097168 | tf_op jit(solution)/shard_map/all_gather | solution.py:84
  140.7 8.3 %while.59 = (s32[]{:T(128)}, f32[512]{0:T(512)S(1)}, f32[512]{0:T(512)S(1)}, f32[512,64]{0,1:T(8,128)S(1)}, s32[4]{0:T(128)S(1)}, /*index=5*/bf16[4,512,128]{2,1...) while((s32[]{:T(128)}, f32[512]{0:T(512)S(1)}, ...), condition=%wide.region_26.27_spmd, body=%wide.region_21.26_spmd.sunk | while | flops 102564864 | bytes 3840275 | solution.py:64
  149.1 8.6 %while.58 = (s32[]{:T(128)}, f32[512]{0:T(512)S(1)}, f32[512]{0:T(512)S(1)}, f32[512,64]{0,1:T(8,128)S(1)}, s32[4]{0:T(128)S(1)}, /*index=5*/bf16[4,512,128]{2,1...) while((s32[]{:T(128)}, f32[512]{0:T(512)S(1)}, ...), condition=%wide.region_20.21_spmd, body=%wide.region_15.20_spmd.sunk | while | flops 102564864 | bytes 3840275 | solution.py:64
  157.8 11.7 %pmax.15 = f32[1024]{0:T(1024)S(1)} all-reduce(f32[1024]{0:T(1024)S(1)} %constant_dynamic-update-slice_fusion.1), channel_id=1, replica_groups=mesh['tgt'=8,'src'=4] {'src'}, use_global_device_ids=true, to_apply=%region_27.28 | all-reduce | flops 1024 | bytes 8192 | tf_op jit(solution)/shard_map/pmax | solution.py:75
  170.3 8.4 %psum.31 = f32[1024]{0:T(1024)S(1)} all-reduce(f32[1024]{0:T(1024)S(1)} %get-tuple-element.636), channel_id=1, replica_groups=mesh['tgt'=8,'src'=4] {'src'}, use_global_device_ids=true, to_apply=%region_29.30 | all-reduce | flops 1024 | bytes 8192 | tf_op jit(solution)/shard_map/psum | solution.py:77
  178.7 23.0 %all-reduce.5.cloned.1.call-done = f32[1024,64]{0,1:T(8,128)} async-done(((f32[1024,64]{0,1:T(8,128)}), f32[1024,64]{0,1:T(8,128)}) %all-reduce.5.cloned.1.call-update) | async-done | bytes 262160 | tf_op jit(solution)/shard_map/psum | solution.py:77
  201.6 1.6 maximum_convert_fusion
  (184 shorter events, 45.0 us)
Async XLA Ops:
  7.2 76.6 %all-reduce.3.cloned.1.call-start = ((), (), s32[]{:S(2)}) async-start(), calls=%async_computation | async-start | bytes 524288 | tf_op jit(solution)/shard_map/psum | solution.py:77
  23.8 59.9 %copy-start.1 = (bf16[1024,64]{0,1:T(8,128)(2,1)S(1)}, bf16[1024,64]{0,1:T(8,128)(2,1)}, u32[]{:S(2)}) copy-start(bf16[1024,64]{0,1:T(8,128)(2,1)} %param.31) | copy-start | bytes 393220
  23.9 63.1 %copy-start.3 = (bf16[2048]{0:T(1024)(128)(2,1)S(1)}, bf16[2048]{0:T(1024)(128)(2,1)}, u32[]{:S(2)}) copy-start(bf16[2048]{0:T(1024)(128)(2,1)} %param.30) | copy-start | bytes 12292
  23.9 63.1 %copy-start = (bf16[1024,128]{1,0:T(8,128)(2,1)S(1)}, bf16[1024,128]{1,0:T(8,128)(2,1)}, u32[]{:S(2)}) copy-start(bf16[1024,128]{1,0:T(8,128)(2,1)} %param.33) | copy-start | bytes 786436
  46.4 63.2 %all-gather.5.cloned.1.call-start = ((), (), s32[]{:S(2)}) async-start(), calls=%async_computation.2 | async-start | bytes 1179648 | tf_op jit(solution)/shard_map/all_gather | solution.py:84
  85.4 54.2 %all-gather.3.cloned.1.call-start = ((), (), s32[]{:S(2)}) async-start(), calls=%async_computation.1 | async-start | bytes 2359296 | tf_op jit(solution)/shard_map/all_gather | solution.py:84
  86.1 115.5 %all-reduce.5.cloned.1.call-start = ((), (), s32[]{:S(2)}) async-start(), calls=%async_computation.3 | async-start | bytes 524288 | tf_op jit(solution)/shard_map/psum | solution.py:77
  149.1 52.5 %copy-start.2 = (bf16[1024,64]{0,1:T(8,128)(2,1)S(1)}, bf16[1024,64]{0,1:T(8,128)(2,1)}, u32[]{:S(2)}) copy-start(bf16[1024,64]{0,1:T(8,128)(2,1)} %param.34) | copy-start | bytes 393220
Sparse Core Ops, SparseCore 0:
  46.6 37.1 all-reduce.2
  86.4 23.2 all-gather.4
  111.7 27.8 all-gather.2
  170.4 31.1 all-reduce.4
where the time goes:
time: 210 us
  waiting for transfers between devices  103 us (49%)
  blocking collectives  38.9 us (19%)
  matrix products  17.6 us (8%)
  local copies, waits for them, and re-layouts  16.8 us (8%)
  between operations  14 us (7%)
  loops' own time  10.9 us (5%)
  other arithmetic  8.22 us (4%)
    all_gather x2, waiting for transfers between devices, regroup(): gathered = lax.all_gather(block_rows, 'tgt', axis=0, tiled=True)  51.3 us
    psum x2, waiting for transfers between devices, finish(): lax.psum((weight_sum * shrink, weighted * shrink[:, None]), 'src')  51.2 us
    pmax x2, blocking collectives, finish(): peak_all = lax.pmax(row_peak, 'src')  21.5 us
    psum x2, blocking collectives, finish(): lax.psum((weight_sum * shrink, weighted * shrink[:, None]), 'src')  17.4 us
    dot_general x16, matrix products, active(): lax.dot_general(target_rows, source_tile, (((1,), (1,)), ((), ())), prefe...  12.4 us
    another operation x4, loops' own time, date_partials(): lax.scan(step, start, (source_tiles, offset_tiles, value_tiles, local_mas...  10.2 us
    dynamic_slice x32, local copies, waits for them, and re-layouts, date_partials(): lax.scan(step, start, (source_tiles, offset_tiles, value_tiles, local_mas...  9.85 us
    dot_general x16, matrix products, active(): jnp.dot(weights.astype(jnp.bfloat16), value_tile, preferred_element_type=...  5.17 us
  transfers between devices with their start and end apart: 4, of which 4 were waited for; matrix products, arithmetic and copies ran while one was open for 1% of the time, Pallas kernels for 0%

commit v1 on v0

v1 whole, which is shorter than its diff:
```python
import functools
import math

import jax
import jax.numpy as jnp
from jax import lax
from jax.experimental import pallas as pl
from jax.experimental.pallas import tpu as pltpu
from jax.sharding import PartitionSpec as P

BLOCK = 512
SHARPNESS = 3.5
LOG2E = math.log2(math.e)
DEAD = 1e30
MESH = pl.DeviceIdType.MESH


def eye(size):
    rows = lax.broadcasted_iota(jnp.int32, (size, size), 0)
    cols = lax.broadcasted_iota(jnp.int32, (size, size), 1)
    return rows == cols


def to_row(column):
    return jnp.sum(jnp.where(eye(column.shape[0]), column, 0.0), axis=0, keepdims=True)


def to_column(row):
    return jnp.sum(jnp.where(eye(row.shape[1]), row, 0.0), axis=1, keepdims=True)


def pack(rows):
    half = rows.shape[0] // 2
    return jnp.concatenate([rows[:half], rows[half:]], axis=1)


def kernel(
    n,
    x1_ref,
    y1_ref,
    h1_ref,
    w1_ref,
    h2_ref,
    e1_ref,
    m1_ref,
    x2_ref,
    e2_ref,
    m2_ref,
    out1_ref,
    out2_ref,
    states,
    offs,
    weights,
    scale2,
    peak_own,
    sum_own,
    acc_own,
    send_w,
    send_s,
    recv_w,
    recv_s,
    gathered,
    far,
    near,
    vals,
    early_pack,
    st_sem,
    off_sem,
    part_send,
    part_recv,
    gat_send,
    gat_recv,
    val_sem,
):
    t = lax.axis_index("tgt")
    s = lax.axis_index("src")
    chip = t // 2
    core = lax.rem(t, 2)
    mate = jnp.bitwise_xor(chip, s)
    partner = 2 * mate + core
    sibling = 2 * chip + 1 - core
    remote = s != 0
    rows_all, width = x1_ref.shape[0], w1_ref.shape[1]
    rows = rows_all // n
    half = rows // 2
    group = min(rows, 128)
    groups = rows // group
    cols = y1_ref.shape[0]
    part = cols // 2
    factor = SHARPNESS / math.sqrt(x1_ref.shape[1]) * LOG2E

    def peer(i):
        return lax.rem(s + i, n)

    barrier = pltpu.get_barrier_semaphore()
    for i in range(1, n):
        pl.semaphore_signal(barrier, inc=1, device_id=(t, peer(i)), device_id_type=MESH)
    pl.semaphore_signal(barrier, inc=1, device_id=(sibling, s), device_id_type=MESH)

    @pl.when(remote)
    def _():
        pl.semaphore_signal(barrier, inc=1, device_id=(partner, s), device_id_type=MESH)

    pl.semaphore_wait(barrier, jnp.where(remote, n + 1, n))

    states_far = pltpu.make_async_remote_copy(
        x1_ref, states.at[0], st_sem.at[0], st_sem.at[1], (partner, s), MESH
    )
    states_here = pltpu.make_async_copy(x1_ref, states.at[0], st_sem.at[0])
    states_near = pltpu.make_async_remote_copy(
        states.at[0], states.at[1], st_sem.at[2], st_sem.at[3], (sibling, s), MESH
    )
    offs_far = pltpu.make_async_remote_copy(h2_ref, offs, off_sem.at[0], off_sem.at[1], (t, mate), MESH)
    offs_here = pltpu.make_async_copy(h2_ref, offs, off_sem.at[0])

    @pl.when(remote)
    def _():
        states_far.start()

    @pl.when(jnp.logical_not(remote))
    def _():
        states_here.start()

    @pl.when(mate != s)
    def _():
        offs_far.start()

    @pl.when(mate == s)
    def _():
        offs_here.start()

    def bias(offset_row, mask_ref, row_tile, col_tile):
        tiles = []
        for c in range(offset_row.shape[1] // BLOCK):
            dead = jnp.where(mask_ref[row_tile, col_tile + c] > 0, 0.0, DEAD)
            tiles.append(offset_row[:, c * BLOCK : (c + 1) * BLOCK] * LOG2E + dead)
        return jnp.concatenate(tiles, axis=1)

    def scores(x, y, bias_row):
        dots = lax.dot_general(x, y, (((1,), (1,)), ((), ())), preferred_element_type=jnp.float32)
        return dots * factor - bias_row

    def part_copies(d, i):
        to = (t, peer(i))
        return (
            pltpu.make_async_remote_copy(
                send_w.at[d, i], recv_w.at[d, i], part_send.at[d, 0, i], part_recv.at[d, 0, i], to, MESH
            ),
            pltpu.make_async_remote_copy(
                send_s.at[d, i], recv_s.at[d, i], part_send.at[d, 1, i], part_recv.at[d, 1, i], to, MESH
            ),
        )

    def ship(d, i, peak, total, acc):
        send_w[d, i] = pack(acc.astype(jnp.bfloat16))
        for g in range(groups):
            send_s[d, i, g : g + 1, 0:group] = to_row(peak[g * group : (g + 1) * group])
            send_s[d, i, 4 + g : 5 + g, 0:group] = to_row(total[g * group : (g + 1) * group])
        for copy in part_copies(d, i):
            copy.start()

    def keep(peak, total, acc):
        peak_own[...] = peak
        sum_own[...] = total
        acc_own[...] = acc

    def combine(d, exercise_ref):
        for i in range(1, n):
            for copy in part_copies(d, i):
                copy.wait_recv()
        peaks, sums = [peak_own[...]], [sum_own[...]]
        for i in range(1, n):
            peaks.append(jnp.concatenate([to_column(recv_s[d, i, g : g + 1, 0:group]) for g in range(groups)], 0))
            sums.append(
                jnp.concatenate([to_column(recv_s[d, i, 4 + g : 5 + g, 0:group]) for g in range(groups)], 0)
            )
        top = functools.reduce(jnp.maximum, peaks)
        shrink = jnp.exp2(peaks[0] - top)
        total = sums[0] * shrink
        acc = acc_own[...] * shrink
        for i in range(1, n):
            shrink = jnp.exp2(peaks[i] - top)
            total = total + sums[i] * shrink
            packed = recv_w[d, i].astype(jnp.float32)
            acc = acc + jnp.concatenate([packed[:, :width], packed[:, width:]], 0) * shrink
        own = pl.ds(pl.multiple_of(s * rows, rows), rows)
        result = jnp.maximum(acc / total, exercise_ref[own, :].astype(jnp.float32))
        return pack(result.astype(jnp.bfloat16))

    def gather_copy(d, buffer, i, slot):
        return pltpu.make_async_remote_copy(
            buffer.at[slot], buffer.at[slot], gat_send.at[d, i], gat_recv.at[d, slot], (t, peer(i)), MESH
        )

    def unpack_to(ref, base, packed):
        ref[pl.ds(pl.multiple_of(base, rows), half), :] = packed[:, :width]
        ref[pl.ds(pl.multiple_of(base + half, half), half), :] = packed[:, width:]

    def first_date(i):
        q = peer(i)
        x = x1_ref[pl.ds(pl.multiple_of(q * rows, rows), rows), :]
        row_tile = (t * rows_all + q * rows) // BLOCK
        sc = scores(x, y1_ref[...], bias(h1_ref[...], m1_ref, row_tile, s * (cols // BLOCK)))
        peak = jnp.max(sc, axis=1, keepdims=True)
        w = jnp.exp2(sc - peak)
        total = jnp.sum(w, axis=1, keepdims=True)
        acc = jnp.dot(w.astype(jnp.bfloat16), w1_ref[...], preferred_element_type=jnp.float32)
        return peak, total, acc

    def first_step(i, carry):
        ship(0, i, *first_date(i))
        return carry

    lax.fori_loop(1, n, first_step, 0)
    keep(*first_date(0))

    @pl.when(remote)
    def _():
        states_far.wait()

    @pl.when(jnp.logical_not(remote))
    def _():
        states_here.wait()

    @pl.when(mate != s)
    def _():
        offs_far.wait()

    @pl.when(mate == s)
    def _():
        offs_here.wait()

    states_near.start()

    def second_weights(k):
        owner = 2 * mate + (core if k == 0 else 1 - core)
        offset_row = offs[:, pl.ds(pl.multiple_of((owner - 2 * mate) * part, part), part)]

        def step(q, carry):
            span = pl.ds(pl.multiple_of(q * rows, rows), rows)
            row_tile = (t * rows_all + q * rows) // BLOCK
            sc = scores(
                x2_ref[span, :],
                states[k],
                bias(offset_row, m2_ref, row_tile, owner * (part // BLOCK)),
            )
            peak = jnp.max(sc, axis=1, keepdims=True)
            w = jnp.exp2(sc - peak)
            weights[k, span, :] = w.astype(jnp.bfloat16)
            scale2[2 * k, span, :] = peak
            scale2[2 * k + 1, span, :] = jnp.sum(w, axis=1, keepdims=True)
            return carry

        lax.fori_loop(0, n, step, 0)

    second_weights(0)

    gathered[s] = combine(0, e1_ref)
    for i in range(1, n):
        gather_copy(0, gathered, i, s).start()

    def far_copy(q):
        return pltpu.make_async_remote_copy(
            gathered.at[q], far.at[q], val_sem.at[0, q], val_sem.at[1, q], (partner, s), MESH
        )

    def here_copy(q):
        return pltpu.make_async_copy(gathered.at[q], far.at[q], val_sem.at[0, q])

    def near_copy(q):
        return pltpu.make_async_remote_copy(
            far.at[q], near.at[q], val_sem.at[2, q], val_sem.at[3, q], (sibling, s), MESH
        )

    def pass_on(q):
        @pl.when(remote)
        def _():
            far_copy(q).start()

        @pl.when(jnp.logical_not(remote))
        def _():
            here_copy(q).start()

    pass_on(s)
    states_near.wait()
    second_weights(1)

    for i in range(1, n):
        gather_copy(0, gathered, i, peer(i)).wait_recv()
        pass_on(peer(i))

    for i in range(n):
        q = peer(i)

        @pl.when(remote)
        def _():
            far_copy(q).wait_recv()

        @pl.when(jnp.logical_not(remote))
        def _():
            here_copy(q).wait()

        near_copy(q).start()
        unpack_to(vals.at[0], q * rows, far[q])
    for i in range(n):
        q = peer(i)
        unpack_to(out1_ref, q * rows, gathered[q])
    for i in range(n):
        q = peer(i)
        near_copy(q).wait_recv()
        unpack_to(vals.at[1], q * rows, near[q])

    def second_date(i):
        span = pl.ds(pl.multiple_of(peer(i) * rows, rows), rows)
        peak0, peak1 = scale2[0, span, :], scale2[2, span, :]
        peak = jnp.maximum(peak0, peak1)
        f0, f1 = jnp.exp2(peak0 - peak), jnp.exp2(peak1 - peak)
        total = f0 * scale2[1, span, :] + f1 * scale2[3, span, :]
        acc = f0 * jnp.dot(weights[0, span, :], vals[0], preferred_element_type=jnp.float32)
        acc = acc + f1 * jnp.dot(weights[1, span, :], vals[1], preferred_element_type=jnp.float32)
        return peak, total, acc

    def second_step(i, carry):
        ship(1, i, *second_date(i))
        return carry

    lax.fori_loop(1, n, second_step, 0)
    keep(*second_date(0))

    early_pack[s] = combine(1, e2_ref)
    for i in range(1, n):
        gather_copy(1, early_pack, i, s).start()
    unpack_to(out2_ref, s * rows, early_pack[s])
    for i in range(1, n):
        q = peer(i)
        gather_copy(1, early_pack, i, q).wait_recv()
        unpack_to(out2_ref, q * rows, early_pack[q])

    for d in range(2):
        for i in range(1, n):
            for copy in part_copies(d, i):
                copy.wait_send()
            gather_copy(d, gathered if d == 0 else early_pack, i, s).wait_send()
    for q in range(n):
        near_copy(q).wait_send()

        @pl.when(remote)
        def _():
            far_copy(q).wait_send()


def per_device(n, states_late, offset_late, values_late, states_mid, offset_mid, exercise_mid, mask_mid,
               states_early, exercise_early, mask_early):
    rows_all, factors = states_mid.shape
    cols, width = values_late.shape
    rows = rows_all // n
    half = rows // 2
    part = cols // 2
    bf16, f32 = jnp.bfloat16, jnp.float32
    vmem = pl.BlockSpec(memory_space=pltpu.VMEM)
    smem = pl.BlockSpec(memory_space=pltpu.SMEM)
    pairs = 2 * rows_all * cols
    call = pl.pallas_call(
        functools.partial(kernel, n),
        out_shape=(
            jax.ShapeDtypeStruct((rows_all, width), bf16),
            jax.ShapeDtypeStruct((rows_all, width), bf16),
        ),
        in_specs=[vmem, vmem, vmem, vmem, vmem, vmem, smem, vmem, vmem, smem],
        out_specs=(vmem, vmem),
        scratch_shapes=[
            pltpu.VMEM((2, rows_all, factors), bf16),
            pltpu.VMEM((1, cols), f32),
            pltpu.VMEM((2, rows_all, part), bf16),
            pltpu.VMEM((4, rows_all, 1), f32),
            pltpu.VMEM((rows, 1), f32),
            pltpu.VMEM((rows, 1), f32),
            pltpu.VMEM((rows, width), f32),
            pltpu.VMEM((2, n, half, 2 * width), bf16),
            pltpu.VMEM((2, n, 8, 128), f32),
            pltpu.VMEM((2, n, half, 2 * width), bf16),
            pltpu.VMEM((2, n, 8, 128), f32),
            pltpu.VMEM((n, half, 2 * width), bf16),
            pltpu.VMEM((n, half, 2 * width), bf16),
            pltpu.VMEM((n, half, 2 * width), bf16),
            pltpu.VMEM((2, part, width), bf16),
            pltpu.VMEM((n, half, 2 * width), bf16),
            pltpu.SemaphoreType.DMA((4,)),
            pltpu.SemaphoreType.DMA((2,)),
            pltpu.SemaphoreType.DMA((2, 2, n)),
            pltpu.SemaphoreType.DMA((2, 2, n)),
            pltpu.SemaphoreType.DMA((2, n)),
            pltpu.SemaphoreType.DMA((2, n)),
            pltpu.SemaphoreType.DMA((4, n)),
        ],
        compiler_params=pltpu.CompilerParams(
            collective_id=0, has_side_effects=True, vmem_limit_bytes=48 * 1024 * 1024
        ),
        cost_estimate=pl.CostEstimate(
            flops=2 * pairs * (factors + width), bytes_accessed=4 * 1024 * 1024, transcendentals=pairs
        ),
    )
    return call(
        states_mid,
        states_late,
        offset_late.astype(f32).reshape(1, cols),
        values_late,
        offset_mid.astype(f32).reshape(1, cols),
        exercise_mid,
        mask_mid,
        states_early,
        exercise_early,
        mask_early,
    )


def solution(mesh):
    in_specs = (
        P("src", None),
        P("src"),
        P("src", None),
        P("tgt", None),
        P("src"),
        P("tgt", None),
        P(),
        P("tgt", None),
        P("tgt", None),
        P(),
    )
    out_specs = (P("tgt", None), P("tgt", None))
    return jax.shard_map(
        functools.partial(per_device, mesh.shape["src"]),
        mesh=mesh,
        in_specs=in_specs,
        out_specs=out_specs,
        check_vma=False,
    )
```

time: 210 us -> 41 us (0.20)
  waiting for transfers between devices: 103 us -> 0 us
  blocking collectives: 38.9 us -> 0 us
  Pallas kernels: 0 us -> 35.5 us
  matrix products: 17.6 us -> 0 us
  between operations: 14 us -> 0.74 us
  local copies, waits for them, and re-layouts: 16.8 us -> 3.92 us
  loops' own time: 10.9 us -> 0 us
  other arithmetic: 8.22 us -> 0.7 us
    all_gather x2 -> x0, waiting for transfers between devices: 51.3 us -> none  [regroup(): gathered = lax.all_gather(block_rows, 'tgt', axis=0, tiled=True)]
    psum x2 -> x0, waiting for transfers between devices: 51.2 us -> none  [finish(): lax.psum((weight_sum * shrink, weighted * shrink[:, None]), 'src')]
    pallas_call x0 -> x1, Pallas kernels: none -> 35.5 us  [per_device(): call(states_mid, states_late, offset_late.astype(f32).reshape(1, cols), v...]
    pmax x2 -> x0, blocking collectives: 21.5 us -> none  [finish(): peak_all = lax.pmax(row_peak, 'src')]
    dot_general x32 -> x0, matrix products: 17.6 us -> none  [the longest x16 12.4 us: active(): lax.dot_general(target_rows, source_tile, (((1,), (1,)), ((), ())), prefe...]
    psum x2 -> x0, blocking collectives: 17.4 us -> none  [finish(): lax.psum((weight_sum * shrink, weighted * shrink[:, None]), 'src')]
    dynamic_slice x36 -> x0, local copies, waits for them, and re-layouts: 13.4 us -> none  [the longest x32 9.85 us: date_partials(): lax.scan(step, start, (source_tiles, offset_tiles, value_tiles, local_mas...]
    another operation x20 -> x0, loops' own time: 10.9 us -> none  [the longest x4 10.2 us: date_partials(): lax.scan(step, start, (source_tiles, offset_tiles, value_tiles, local_mas...]
  transfers between devices with their start and end apart: 4 -> 0, of which waited for: 4 -> 0; matrix products, arithmetic and copies ran while one was open for 1% -> 0% of each run, Pallas kernels for 0% -> 0%
where the time goes in v1:
time: 41 us; the launch traced here: 40.8 us
  Pallas kernels  35.5 us (87%)
  local copies, waits for them, and re-layouts  3.92 us (10%)
  between operations  0.74 us (2%)
  other arithmetic  0.7 us (2%)
    pallas_call x1, Pallas kernels, per_device(): call(states_mid, states_late, offset_late.astype(f32).reshape(1, cols), v...  35.5 us
    unnamed x19, local copies, waits for them, and re-layouts  2.34 us
    pallas_call x2, local copies, waits for them, and re-layouts, per_device(): call(states_mid, states_late, offset_late.astype(f32).reshape(1, cols), v...  1.57 us

profile of v1, /device:TPU:0, one launch (start us, length us, event | category | flops | bytes accessed | tf_op | source)
XLA Modules:
  0.0 40.8 jit_solution(16333158261264253608)
XLA Ops:
  0.6 0.0 copy-start.7
  0.6 0.7 %reshape.18 = f32[2048]{0:T(1024)S(1)} convert(bf16[2048]{0:T(1024)(128)(2,1)} %param.11) | non-fusion elementwise | flops 2048 | bytes 12288 | tf_op jit(solution)/shard_map/reshape | solution.py:406
  1.3 0.0 copy-done.7
  1.3 0.0 copy-start.6
  1.3 0.0 copy-start.5
  1.4 1.1 %copy.13.e1_ref = bf16[1024,64]{1,0:T(8,128)(2,1)S(1)} copy(bf16[1024,64]{0,1:T(8,128)(2,1)} %param.15) | data formatting | bytes 262144 | tf_op args[5]
  2.5 0.0 copy-done.6
  2.5 0.0 copy-start
  2.5 0.2 copy.14.e2_ref
  2.7 0.0 copy-done.5
  2.7 0.0 copy-start.1
  2.7 0.0 copy-start.2
  2.7 0.0 copy-start.3
  2.7 0.0 copy-start.4
  2.7 0.3 copy.12.w1_ref
  3.0 0.5 %copy-done = bf16[2048,128]{1,0:T(8,128)(2,1)S(1)} copy-done((bf16[2048,128]{1,0:T(8,128)(2,1)S(1)}, bf16[2048,128]{1,0:T(8,128)(2,1)}, u32[]{:S(2)}) %copy-start) | copy-done | bytes 524312
  3.5 0.1 copy-done.1
  3.7 0.1 copy-done.2
  3.8 0.0 copy-done.3
  3.8 0.0 copy-done.4
  3.8 35.5 %shard_map.113 = (bf16[1024,64]{1,0:T(8,128)(2,1)S(1)}, bf16[1024,64]{1,0:T(8,128)(2,1)S(1)}) custom-call(bf16[1024,128]{1,0:T(8,128)(2,1)S(1)} %copy-done.1, bf16[2048,128]{1,0:T(8,128)(2,1)S(1)} %copy-done, f32[1,2048]{1,0:T(1,128)S(1)} %bitcast.2, bf16[2048,64]{1,0:T(8,128)(2,1)S(1)} %copy.12.w1_ref, f32[1,2048]{1,0:T(1,128)S(1)} %bitcast.3, ...), custom_call_target="tpu_custom_call" | custom-call | flops 1610612736 | bytes 4194304 | tf_op jit(solution)/shard_map/pallas_call | solution.py:403
  39.2 0.8 %copy.15 = bf16[1024,64]{0,1:T(8,128)(2,1)} copy(bf16[1024,64]{1,0:T(8,128)(2,1)S(1)} %get-tuple-element.2) | data formatting | bytes 262144 | tf_op jit(solution)/shard_map/pallas_call | solution.py:403
  40.0 0.8 %copy.16 = bf16[1024,64]{0,1:T(8,128)(2,1)} copy(bf16[1024,64]{1,0:T(8,128)(2,1)S(1)} %get-tuple-element.3) | data formatting | bytes 262144 | tf_op jit(solution)/shard_map/pallas_call | solution.py:403
  (1 shorter events, 0.0 us)
Async XLA Ops:
  0.6 0.7 %copy-start.7 = (bf16[2048]{0:T(1024)(128)(2,1)S(1)}, bf16[2048]{0:T(1024)(128)(2,1)}, u32[]{:S(2)}) copy-start(bf16[2048]{0:T(1024)(128)(2,1)} %param.14) | copy-start | bytes 12292
  1.3 1.1 %copy-start.6 = (bf16[1024,64]{0,1:T(8,128)(2,1)S(1)}, bf16[1024,64]{0,1:T(8,128)(2,1)}, u32[]{:S(2)}) copy-start(bf16[1024,64]{0,1:T(8,128)(2,1)} %param.18) | copy-start | bytes 393220
  1.3 1.3 %copy-start.5 = (bf16[2048,64]{0,1:T(8,128)(2,1)S(1)}, bf16[2048,64]{0,1:T(8,128)(2,1)}, u32[]{:S(2)}) copy-start(bf16[2048,64]{0,1:T(8,128)(2,1)} %param.12) | copy-start | bytes 786436
  2.5 1.0 %copy-start = (bf16[2048,128]{1,0:T(8,128)(2,1)S(1)}, bf16[2048,128]{1,0:T(8,128)(2,1)}, u32[]{:S(2)}) copy-start(bf16[2048,128]{1,0:T(8,128)(2,1)} %y1_ref.1) | copy-start | bytes 1572868
  2.7 1.0 %copy-start.1 = (bf16[1024,128]{1,0:T(8,128)(2,1)S(1)}, bf16[1024,128]{1,0:T(8,128)(2,1)}, u32[]{:S(2)}) copy-start(bf16[1024,128]{1,0:T(8,128)(2,1)} %x1_ref.1) | copy-start | bytes 786436
  2.7 1.1 %copy-start.2 = (bf16[1024,128]{1,0:T(8,128)(2,1)S(1)}, bf16[1024,128]{1,0:T(8,128)(2,1)}, u32[]{:S(2)}) copy-start(bf16[1024,128]{1,0:T(8,128)(2,1)} %x2_ref.1) | copy-start | bytes 786436
  2.7 1.0 %copy-start.3 = (s32[16,16]{1,0:T(8,128)S(1)}, s32[16,16]{1,0:T(8,128)}, u32[]{:S(2)}) copy-start(s32[16,16]{1,0:T(8,128)} %m1_ref.1) | copy-start | bytes 3076
  2.7 1.0 %copy-start.4 = (s32[16,16]{1,0:T(8,128)S(1)}, s32[16,16]{1,0:T(8,128)}, u32[]{:S(2)}) copy-start(s32[16,16]{1,0:T(8,128)} %m2_ref.1) | copy-start | bytes 3076

commit v2 on v1

v2 whole, which is shorter than its diff:
```python
import functools
import math

import jax
import jax.numpy as jnp
from jax import lax
from jax.experimental import pallas as pl
from jax.experimental.pallas import tpu as pltpu
from jax.sharding import PartitionSpec as P

BLOCK = 512
SHARPNESS = 3.5
LOG2E = math.log2(math.e)
DEAD = 1e30
MESH = pl.DeviceIdType.MESH


def kernel(
    n,
    x1_hbm,
    y1_hbm,
    h1_ref,
    w1_hbm,
    h2_ref,
    e1_hbm,
    m1_ref,
    x2_hbm,
    e2_hbm,
    m2_ref,
    out1_ref,
    out2_ref,
    x1_ref,
    y1_ref,
    w1_ref,
    e1_ref,
    x2_ref,
    e2_ref,
    states,
    offs,
    bias_ref,
    weights,
    peaks2,
    sums2,
    peak_own,
    sum_own,
    acc_own,
    send_w,
    send_s,
    recv_w,
    recv_s,
    gathered,
    far,
    near,
    vals,
    early,
    in_sem,
    st_sem,
    off_sem,
    part_send,
    part_recv,
    gat_send,
    gat_recv,
    val_sem,
):
    t = lax.axis_index("tgt")
    s = lax.axis_index("src")
    chip = t // 2
    core = lax.rem(t, 2)
    mate = jnp.bitwise_xor(chip, s)
    partner = 2 * mate + core
    sibling = 2 * chip + 1 - core
    remote = s != 0
    rows_all, width = x1_ref.shape[0], w1_ref.shape[0]
    rows = rows_all // n
    cols = y1_ref.shape[0]
    part = cols // 2
    factor = SHARPNESS / math.sqrt(x1_ref.shape[1]) * LOG2E

    def peer(i):
        return lax.rem(s + i, n)

    fetches = [
        pltpu.make_async_copy(a, b, in_sem.at[k])
        for k, (a, b) in enumerate(
            [(x1_hbm, x1_ref), (y1_hbm, y1_ref), (w1_hbm, w1_ref), (e1_hbm, e1_ref), (x2_hbm, x2_ref), (e2_hbm, e2_ref)]
        )
    ]
    for fetch in fetches:
        fetch.start()

    barrier = pltpu.get_barrier_semaphore()
    for i in range(1, n):
        pl.semaphore_signal(barrier, inc=1, device_id=(t, peer(i)), device_id_type=MESH)
    pl.semaphore_signal(barrier, inc=1, device_id=(sibling, s), device_id_type=MESH)

    @pl.when(remote)
    def _():
        pl.semaphore_signal(barrier, inc=1, device_id=(partner, s), device_id_type=MESH)

    def bias_columns(offset_row):
        full = jnp.broadcast_to(offset_row * LOG2E, (128, offset_row.shape[1]))
        return jnp.transpose(full)

    bias_ref[0] = bias_columns(h1_ref[...])
    pl.semaphore_wait(barrier, jnp.where(remote, n + 1, n))

    states_far = pltpu.make_async_remote_copy(
        x1_ref, states.at[0], st_sem.at[0], st_sem.at[1], (partner, s), MESH
    )
    states_here = pltpu.make_async_copy(x1_ref, states.at[0], st_sem.at[0])
    states_near = pltpu.make_async_remote_copy(
        states.at[0], states.at[1], st_sem.at[2], st_sem.at[3], (sibling, s), MESH
    )
    offs_far = pltpu.make_async_remote_copy(h2_ref, offs, off_sem.at[0], off_sem.at[1], (t, mate), MESH)
    offs_here = pltpu.make_async_copy(h2_ref, offs, off_sem.at[0])
    fetches[0].wait()

    @pl.when(remote)
    def _():
        states_far.start()

    @pl.when(jnp.logical_not(remote))
    def _():
        states_here.start()

    @pl.when(mate != s)
    def _():
        offs_far.start()

    @pl.when(mate == s)
    def _():
        offs_here.start()

    def softmax_part(y, x, bias, mask_ref, row_tile, col_tile):
        dots = lax.dot_general(y, x, (((1,), (1,)), ((), ())), preferred_element_type=jnp.float32)
        if rows >= 128:
            wide = jnp.concatenate([bias] * (rows // 128), axis=1)
        else:
            wide = bias[:, :rows]
        sc = dots * factor - wide
        tiles = [sc[c * BLOCK : (c + 1) * BLOCK] for c in range(sc.shape[0] // BLOCK)]
        live = [mask_ref[row_tile, col_tile + c] > 0 for c in range(len(tiles))]
        tops = [jnp.max(tile, axis=0, keepdims=True) for tile in tiles]
        peak = functools.reduce(jnp.maximum, [jnp.where(a, b, -DEAD) for a, b in zip(live, tops)])
        w = [jnp.exp2(tile - jnp.where(a, peak, DEAD)) for a, tile in zip(live, tiles)]
        total = functools.reduce(jnp.add, [jnp.sum(tile, axis=0, keepdims=True) for tile in w])
        return peak, total, jnp.concatenate([tile.astype(jnp.bfloat16) for tile in w], axis=0)

    def part_copies(d, i):
        to = (t, peer(i))
        return (
            pltpu.make_async_remote_copy(
                send_w.at[d, i], recv_w.at[d, i], part_send.at[d, 0, i], part_recv.at[d, 0, i], to, MESH
            ),
            pltpu.make_async_remote_copy(
                send_s.at[d, i], recv_s.at[d, i], part_send.at[d, 1, i], part_recv.at[d, 1, i], to, MESH
            ),
        )

    def ship(d, i, peak, total, acc):
        send_w[d, i] = acc.astype(jnp.bfloat16)
        send_s[d, i, 0:1, :] = peak
        send_s[d, i, 1:2, :] = total
        for copy in part_copies(d, i):
            copy.start()

    def keep(peak, total, acc):
        peak_own[...] = peak
        sum_own[...] = total
        acc_own[...] = acc

    def own_columns(ref):
        if rows % 128 == 0:
            return ref[:, pl.ds(pl.multiple_of(s * rows, rows), rows)].astype(jnp.float32)
        picked = jnp.zeros((width, rows), jnp.float32)
        for q in range(n):
            picked = jnp.where(s == q, ref[:, q * rows : (q + 1) * rows].astype(jnp.float32), picked)
        return picked

    def combine(d, exercise_ref):
        for i in range(1, n):
            for copy in part_copies(d, i):
                copy.wait_recv()
        peaks = [peak_own[...]] + [recv_s[d, i, 0:1, :] for i in range(1, n)]
        sums = [sum_own[...]] + [recv_s[d, i, 1:2, :] for i in range(1, n)]
        top = functools.reduce(jnp.maximum, peaks)
        shrink = jnp.exp2(peaks[0] - top)
        total = sums[0] * shrink
        acc = acc_own[...] * shrink
        for i in range(1, n):
            shrink = jnp.exp2(peaks[i] - top)
            total = total + sums[i] * shrink
            acc = acc + recv_w[d, i].astype(jnp.float32) * shrink
        return jnp.maximum(acc / total, own_columns(exercise_ref)).astype(jnp.bfloat16)

    def gather_copy(d, buffer, i, slot):
        return pltpu.make_async_remote_copy(
            buffer.at[slot], buffer.at[slot], gat_send.at[d, i], gat_recv.at[d, slot], (t, peer(i)), MESH
        )

    def first_date(i):
        q = peer(i)
        x = x1_ref[pl.ds(pl.multiple_of(q * rows, rows), rows), :]
        row_tile = (t * rows_all + q * rows) // BLOCK
        peak, total, w = softmax_part(y1_ref[...], x, bias_ref[0], m1_ref, row_tile, s * (cols // BLOCK))
        return peak, total, jnp.dot(w1_ref[...], w, preferred_element_type=jnp.float32)

    def first_step(i, carry):
        ship(0, i, *first_date(i))
        return carry

    for fetch in fetches[1:]:
        fetch.wait()
    lax.fori_loop(1, n, first_step, 0)
    keep(*first_date(0))

    gathered[s] = combine(0, e1_ref)
    for i in range(1, n):
        gather_copy(0, gathered, i, s).start()

    def far_copy(q):
        return pltpu.make_async_remote_copy(
            gathered.at[q], far.at[q], val_sem.at[0, q], val_sem.at[1, q], (partner, s), MESH
        )

    def here_copy(q):
        return pltpu.make_async_copy(gathered.at[q], far.at[q], val_sem.at[0, q])

    def near_copy(q):
        return pltpu.make_async_remote_copy(
            far.at[q], near.at[q], val_sem.at[2, q], val_sem.at[3, q], (sibling, s), MESH
        )

    def pass_on(q):
        @pl.when(remote)
        def _():
            far_copy(q).start()

        @pl.when(jnp.logical_not(remote))
        def _():
            here_copy(q).start()

    def pass_near(q):
        @pl.when(remote)
        def _():
            far_copy(q).wait_recv()

        @pl.when(jnp.logical_not(remote))
        def _():
            here_copy(q).wait()

        near_copy(q).start()

    pass_on(s)

    @pl.when(remote)
    def _():
        states_far.wait()

    @pl.when(jnp.logical_not(remote))
    def _():
        states_here.wait()

    @pl.when(mate != s)
    def _():
        offs_far.wait()

    @pl.when(mate == s)
    def _():
        offs_here.wait()

    states_near.start()
    bias_ref[1] = bias_columns(offs[...])

    def second_weights(k, low, high):
        place = core if k == 0 else 1 - core
        owner = 2 * mate + place

        def step(q, carry):
            span = pl.ds(pl.multiple_of(q * rows, rows), rows)
            row_tile = (t * rows_all + q * rows) // BLOCK
            bias = bias_ref[1, pl.ds(pl.multiple_of(place * part, part), part), :]
            peak, total, w = softmax_part(
                states[k], x2_ref[span, :], bias, m2_ref, row_tile, owner * (part // BLOCK)
            )
            weights[k, q] = w
            peaks2[k, q] = peak
            sums2[k, q] = total
            return carry

        lax.fori_loop(low, high, step, 0)

    second_weights(0, 0, n)
    states_near.wait()
    for i in range(1, n):
        gather_copy(0, gathered, i, peer(i)).wait_recv()
        pass_on(peer(i))
        second_weights(1, i - 1, i)
    pass_near(s)
    second_weights(1, n - 1, n)
    for i in range(1, n):
        pass_near(peer(i))
    for q in range(n):
        out1_ref[:, q * rows : (q + 1) * rows] = gathered[q]
        vals[0, :, q * rows : (q + 1) * rows] = far[q]
    for q in range(n):
        near_copy(q).wait_recv()
        vals[1, :, q * rows : (q + 1) * rows] = near[q]

    def second_date(i):
        q = peer(i)
        peak0, peak1 = peaks2[0, q], peaks2[1, q]
        peak = jnp.maximum(peak0, peak1)
        f0, f1 = jnp.exp2(peak0 - peak), jnp.exp2(peak1 - peak)
        total = f0 * sums2[0, q] + f1 * sums2[1, q]
        acc = f0 * jnp.dot(vals[0], weights[0, q], preferred_element_type=jnp.float32)
        acc = acc + f1 * jnp.dot(vals[1], weights[1, q], preferred_element_type=jnp.float32)
        return peak, total, acc

    def second_step(i, carry):
        ship(1, i, *second_date(i))
        return carry

    lax.fori_loop(1, n, second_step, 0)
    keep(*second_date(0))

    early[s] = combine(1, e2_ref)
    for i in range(1, n):
        gather_copy(1, early, i, s).start()
    for i in range(1, n):
        gather_copy(1, early, i, peer(i)).wait_recv()
    for q in range(n):
        out2_ref[:, q * rows : (q + 1) * rows] = early[q]

    for d in range(2):
        for i in range(1, n):
            for copy in part_copies(d, i):
                copy.wait_send()
            gather_copy(d, gathered if d == 0 else early, i, s).wait_send()
    for q in range(n):
        near_copy(q).wait_send()

        @pl.when(remote)
        def _():
            far_copy(q).wait_send()


def per_device(n, states_late, offset_late, values_late, states_mid, offset_mid, exercise_mid, mask_mid,
               states_early, exercise_early, mask_early):
    rows_all, factors = states_mid.shape
    cols, width = values_late.shape
    rows = rows_all // n
    part = cols // 2
    bf16, f32 = jnp.bfloat16, jnp.float32
    vmem = pl.BlockSpec(memory_space=pltpu.VMEM)
    smem = pl.BlockSpec(memory_space=pltpu.SMEM)
    hbm = pl.BlockSpec(memory_space=pltpu.HBM)
    pairs = 2 * rows_all * cols
    call = pl.pallas_call(
        functools.partial(kernel, n),
        out_shape=(
            jax.ShapeDtypeStruct((width, rows_all), bf16),
            jax.ShapeDtypeStruct((width, rows_all), bf16),
        ),
        in_specs=[hbm, hbm, vmem, hbm, vmem, hbm, smem, hbm, hbm, smem],
        out_specs=(vmem, vmem),
        scratch_shapes=[
            pltpu.VMEM((rows_all, factors), bf16),
            pltpu.VMEM((cols, factors), bf16),
            pltpu.VMEM((width, cols), bf16),
            pltpu.VMEM((width, rows_all), bf16),
            pltpu.VMEM((rows_all, factors), bf16),
            pltpu.VMEM((width, rows_all), bf16),
            pltpu.VMEM((2, rows_all, factors), bf16),
            pltpu.VMEM((1, cols), f32),
            pltpu.VMEM((2, cols, 128), f32),
            pltpu.VMEM((2, n, part, rows), bf16),
            pltpu.VMEM((2, n, 1, rows), f32),
            pltpu.VMEM((2, n, 1, rows), f32),
            pltpu.VMEM((1, rows), f32),
            pltpu.VMEM((1, rows), f32),
            pltpu.VMEM((width, rows), f32),
            pltpu.VMEM((2, n, width, rows), bf16),
            pltpu.VMEM((2, n, 2, rows), f32),
            pltpu.VMEM((2, n, width, rows), bf16),
            pltpu.VMEM((2, n, 2, rows), f32),
            pltpu.VMEM((n, width, rows), bf16),
            pltpu.VMEM((n, width, rows), bf16),
            pltpu.VMEM((n, width, rows), bf16),
            pltpu.VMEM((2, width, part), bf16),
            pltpu.VMEM((n, width, rows), bf16),
            pltpu.SemaphoreType.DMA((6,)),
            pltpu.SemaphoreType.DMA((4,)),
            pltpu.SemaphoreType.DMA((2,)),
            pltpu.SemaphoreType.DMA((2, 2, n)),
            pltpu.SemaphoreType.DMA((2, 2, n)),
            pltpu.SemaphoreType.DMA((2, n)),
            pltpu.SemaphoreType.DMA((2, n)),
            pltpu.SemaphoreType.DMA((4, n)),
        ],
        compiler_params=pltpu.CompilerParams(
            collective_id=0, has_side_effects=True, vmem_limit_bytes=62 * 1024 * 1024
        ),
        cost_estimate=pl.CostEstimate(
            flops=2 * pairs * (factors + width), bytes_accessed=4 * 1024 * 1024, transcendentals=pairs
        ),
    )
    value_mid, value_early = call(
        states_mid,
        states_late,
        offset_late.astype(f32).reshape(1, cols),
        values_late.T,
        offset_mid.astype(f32).reshape(1, cols),
        exercise_mid.T,
        mask_mid,
        states_early,
        exercise_early.T,
        mask_early,
    )
    return value_mid.T, value_early.T


def solution(mesh):
    in_specs = (
        P("src", None),
        P("src"),
        P("src", None),
        P("tgt", None),
        P("src"),
        P("tgt", None),
        P(),
        P("tgt", None),
        P("tgt", None),
        P(),
    )
    out_specs = (P("tgt", None), P("tgt", None))
    return jax.shard_map(
        functools.partial(per_device, mesh.shape["src"]),
        mesh=mesh,
        in_specs=in_specs,
        out_specs=out_specs,
        check_vma=False,
    )
```

time: 41 us -> 38.2 us (0.932)
  Pallas kernels: 35.5 us -> 32.9 us
  local copies, waits for them, and re-layouts: 3.92 us -> 3.03 us
  other arithmetic: 0.7 us -> 1.2 us
    pallas_call x1, Pallas kernels: 35.5 us -> 32.9 us  [per_device(): call(states_mid, states_late, offset_late.astype(f32).reshape(1, cols), v...]
    pallas_call x2 -> x0, local copies, waits for them, and re-layouts: 1.57 us -> none  [per_device(): call(states_mid, states_late, offset_late.astype(f32).reshape(1, cols), v...]
    unnamed x19 -> x8, local copies, waits for them, and re-layouts: 2.34 us -> 3.03 us
    reshape x1, other arithmetic: 0.01 us -> 0.6 us  [per_device(): offset_mid.astype(f32).reshape(1, cols)]
where the time goes in v2:
time: 38.2 us; the launch traced here: 37.8 us
  Pallas kernels  32.9 us (86%)
  local copies, waits for them, and re-layouts  3.03 us (8%)
  other arithmetic  1.2 us (3%)
  between operations  0.66 us (2%)
    pallas_call x1, Pallas kernels, per_device(): call(states_mid, states_late, offset_late.astype(f32).reshape(1, cols), v...  32.9 us
    unnamed x8, local copies, waits for them, and re-layouts  3.03 us

profile of v2, /device:TPU:0, one launch (start us, length us, event | category | flops | bytes accessed | tf_op | source)
XLA Modules:
  0.0 37.8 jit_solution(12871789799287552400)
XLA Ops:
  0.6 0.0 copy-start.1
  0.6 0.7 %copy-done.1 = bf16[2048]{0:T(1024)(128)(2,1)S(1)} copy-done((bf16[2048]{0:T(1024)(128)(2,1)S(1)}, bf16[2048]{0:T(1024)(128)(2,1)}, u32[]{:S(2)}) %copy-start.1) | copy-done | bytes 4120
  1.3 0.0 copy-start.2
  1.3 0.6 %reshape.18 = f32[2048]{0:T(1024)} convert(bf16[2048]{0:T(1024)(128)(2,1)S(1)} %copy-done.1) | non-fusion elementwise | flops 2048 | bytes 12288 | tf_op jit(solution)/shard_map/reshape | solution.py:411
  1.9 0.1 copy-done.2
  2.0 0.6 %reshape.20 = f32[2048]{0:T(1024)} convert(bf16[2048]{0:T(1024)(128)(2,1)S(1)} %copy-done.2) | non-fusion elementwise | flops 2048 | bytes 12288 | tf_op jit(solution)/shard_map/reshape | solution.py:413
  2.6 32.9 %shard_map.113 = (bf16[64,1024]{1,0:T(8,128)(2,1)}, bf16[64,1024]{1,0:T(8,128)(2,1)}) custom-call(bf16[1024,128]{1,0:T(8,128)(2,1)} %x1_hbm.1, bf16[2048,128]{1,0:T(8,128)(2,1)} %y1_hbm.1, f32[1,2048]{1,0:T(1,128)} %bitcast.9, bf16[64,2048]{1,0:T(8,128)(2,1)} %bitcast.11, f32[1,2048]{1,0:T(1,128)} %bitcast.10, bf16[64,1024]{1,0:T(8,128)(2,1)} %bitcast.12, ...), custom_call_target="tpu_custom_call" | custom-call | flops 1610612736 | bytes 4194304 | tf_op jit(solution)/shard_map/pallas_call | solution.py:408
  35.6 0.0 copy-start
  35.6 1.6 %copy.14 = bf16[1024,64]{0,1:T(8,128)(2,1)} copy(bf16[1024,64]{0,1:T(8,128)(2,1)} %bitcast.8) | data formatting | bytes 262144
  37.2 0.0 copy-done
  37.2 0.7 %copy.15 = bf16[1024,64]{0,1:T(8,128)(2,1)} copy(bf16[1024,64]{0,1:T(8,128)(2,1)S(1)} %bitcast.7) | data formatting | bytes 262144
Async XLA Ops:
  0.6 0.7 %copy-start.1 = (bf16[2048]{0:T(1024)(128)(2,1)S(1)}, bf16[2048]{0:T(1024)(128)(2,1)}, u32[]{:S(2)}) copy-start(bf16[2048]{0:T(1024)(128)(2,1)} %param.11) | copy-start | bytes 12292
  1.3 0.7 %copy-start.2 = (bf16[2048]{0:T(1024)(128)(2,1)S(1)}, bf16[2048]{0:T(1024)(128)(2,1)}, u32[]{:S(2)}) copy-start(bf16[2048]{0:T(1024)(128)(2,1)} %param.14) | copy-start | bytes 12292
  35.6 1.6 %copy-start = (bf16[64,1024]{1,0:T(8,128)(2,1)S(1)}, bf16[64,1024]{1,0:T(8,128)(2,1)}, u32[]{:S(2)}) copy-start(bf16[64,1024]{1,0:T(8,128)(2,1)} %get-tuple-element.5) | copy-start | bytes 393220

commit v3 on v2

--- a/solution.py
+++ b/solution.py
@@ -19,9 +19,8 @@
     n,
     x1_hbm,
     y1_hbm,
-    h1_ref,
+    h_ref,
     w1_hbm,
-    h2_ref,
     e1_hbm,
     m1_ref,
     x2_hbm,
@@ -101,7 +100,7 @@
         full = jnp.broadcast_to(offset_row * LOG2E, (128, offset_row.shape[1]))
         return jnp.transpose(full)
 
-    bias_ref[0] = bias_columns(h1_ref[...])
+    bias_ref[0] = bias_columns(h_ref[0])
     pl.semaphore_wait(barrier, jnp.where(remote, n + 1, n))
 
     states_far = pltpu.make_async_remote_copy(
@@ -111,8 +110,8 @@
     states_near = pltpu.make_async_remote_copy(
         states.at[0], states.at[1], st_sem.at[2], st_sem.at[3], (sibling, s), MESH
     )
-    offs_far = pltpu.make_async_remote_copy(h2_ref, offs, off_sem.at[0], off_sem.at[1], (t, mate), MESH)
-    offs_here = pltpu.make_async_copy(h2_ref, offs, off_sem.at[0])
+    offs_far = pltpu.make_async_remote_copy(h_ref.at[1], offs, off_sem.at[0], off_sem.at[1], (t, mate), MESH)
+    offs_here = pltpu.make_async_copy(h_ref.at[1], offs, off_sem.at[0])
     fetches[0].wait()
 
     @pl.when(remote)
@@ -209,11 +208,13 @@
         ship(0, i, *first_date(i))
         return carry
 
-    for fetch in fetches[1:]:
-        fetch.wait()
+    fetches[1].wait()
+    fetches[2].wait()
     lax.fori_loop(1, n, first_step, 0)
     keep(*first_date(0))
 
+    for fetch in fetches[3:]:
+        fetch.wait()
     gathered[s] = combine(0, e1_ref)
     for i in range(1, n):
         gather_copy(0, gathered, i, s).start()
@@ -362,7 +363,7 @@
             jax.ShapeDtypeStruct((width, rows_all), bf16),
             jax.ShapeDtypeStruct((width, rows_all), bf16),
         ),
-        in_specs=[hbm, hbm, vmem, hbm, vmem, hbm, smem, hbm, hbm, smem],
+        in_specs=[hbm, hbm, vmem, hbm, hbm, smem, hbm, hbm, smem],
         out_specs=(vmem, vmem),
         scratch_shapes=[
             pltpu.VMEM((rows_all, factors), bf16),
@@ -408,9 +409,8 @@
     value_mid, value_early = call(
         states_mid,
         states_late,
-        offset_late.astype(f32).reshape(1, cols),
+        jnp.stack([offset_late, offset_mid]).astype(f32).reshape(2, 1, cols),
         values_late.T,
-        offset_mid.astype(f32).reshape(1, cols),
         exercise_mid.T,
         mask_mid,
         states_early,

time: 38.2 us -> 38.2 us (level)
  local copies, waits for them, and re-layouts: 3.03 us -> 3.63 us
  other arithmetic: 1.2 us -> 0.63 us
    reshape x2 -> x0, other arithmetic: 1.2 us -> none  [the longest x1 0.6 us: per_device(): offset_late.astype(f32).reshape(1, cols)]
    convert_element_type x0 -> x1, other arithmetic: none -> 0.63 us  [per_device(): jnp.stack([offset_late, offset_mid]).astype(f32).reshape(2, 1, cols)]
    unnamed x8, local copies, waits for them, and re-layouts: 3.03 us -> 3.62 us
where the time goes in v3:
time: 38.2 us; the launch traced here: 37.8 us
  Pallas kernels  32.9 us (86%)
  local copies, waits for them, and re-layouts  3.63 us (10%)
  between operations  0.66 us (2%)
  other arithmetic  0.63 us (2%)
    pallas_call x1, Pallas kernels, per_device(): call(states_mid, states_late, jnp.stack([offset_late, offset_mid]).astype...  32.9 us
    unnamed x8, local copies, waits for them, and re-layouts  3.62 us

profile of v3, /device:TPU:0, one launch (start us, length us, event | category | flops | bytes accessed | tf_op | source)
XLA Modules:
  0.0 37.8 jit_solution(8838504464488060467)
XLA Ops:
  0.6 0.0 copy-start.1
  0.6 0.7 %copy-done.1 = bf16[2048]{0:T(1024)(128)(2,1)S(1)} copy-done((bf16[2048]{0:T(1024)(128)(2,1)S(1)}, bf16[2048]{0:T(1024)(128)(2,1)}, u32[]{:S(2)}) %copy-start.1) | copy-done | bytes 4120
  1.3 0.0 copy-start.2
  1.3 0.7 %copy-done.2 = bf16[2048]{0:T(1024)(128)(2,1)S(1)} copy-done((bf16[2048]{0:T(1024)(128)(2,1)S(1)}, bf16[2048]{0:T(1024)(128)(2,1)}, u32[]{:S(2)}) %copy-start.2) | copy-done | bytes 4120
  2.0 0.6 %maximum_convert_fusion.h_ref = f32[2,1,2048]{2,1,0:T(1,128)} fusion(bf16[1,1,2048]{2,1,0:T(2,128)(2,1)S(1)} %stack.10, bf16[1,1,2048]{2,1,0:T(2,128)(2,1)S(1)} %stack.9), kind=kLoop, calls=%fused_computation | loop fusion | flops 8192 | bytes 24576 | tf_op jit(solution)/shard_map/convert_element_type | solution.py:412
  2.6 32.9 %shard_map.113 = (bf16[64,1024]{1,0:T(8,128)(2,1)}, bf16[64,1024]{1,0:T(8,128)(2,1)}) custom-call(bf16[1024,128]{1,0:T(8,128)(2,1)} %x1_hbm.1, bf16[2048,128]{1,0:T(8,128)(2,1)} %y1_hbm.1, f32[2,1,2048]{2,1,0:T(1,128)} %maximum_convert_fusion.h_ref, bf16[64,2048]{1,0:T(8,128)(2,1)} %bitcast.7, bf16[64,1024]{1,0:T(8,128)(2,1)} %bitcast.8, s32[16,16]{1,0:T(8,128)} %m1_ref.1, ...), custom_call_target="tpu_custom_call" | custom-call | flops 1610612736 | bytes 4194304 | tf_op jit(solution)/shard_map/pallas_call | solution.py:409
  35.6 0.0 copy-start
  35.6 1.6 %copy.14 = bf16[1024,64]{0,1:T(8,128)(2,1)} copy(bf16[1024,64]{0,1:T(8,128)(2,1)} %bitcast.6) | data formatting | bytes 262144
  37.2 0.0 copy-done
  37.2 0.7 %copy.15 = bf16[1024,64]{0,1:T(8,128)(2,1)} copy(bf16[1024,64]{0,1:T(8,128)(2,1)S(1)} %bitcast.5) | data formatting | bytes 262144
  (2 shorter events, 0.0 us)
Async XLA Ops:
  0.6 0.7 %copy-start.1 = (bf16[2048]{0:T(1024)(128)(2,1)S(1)}, bf16[2048]{0:T(1024)(128)(2,1)}, u32[]{:S(2)}) copy-start(bf16[2048]{0:T(1024)(128)(2,1)} %param.11) | copy-start | bytes 12292
  1.3 0.7 %copy-start.2 = (bf16[2048]{0:T(1024)(128)(2,1)S(1)}, bf16[2048]{0:T(1024)(128)(2,1)}, u32[]{:S(2)}) copy-start(bf16[2048]{0:T(1024)(128)(2,1)} %param.14) | copy-start | bytes 12292
  35.6 1.6 %copy-start = (bf16[64,1024]{1,0:T(8,128)(2,1)S(1)}, bf16[64,1024]{1,0:T(8,128)(2,1)}, u32[]{:S(2)}) copy-start(bf16[64,1024]{1,0:T(8,128)(2,1)} %get-tuple-element.5) | copy-start | bytes 393220

commit v4 on v2

--- a/solution.py
+++ b/solution.py
@@ -321,7 +321,7 @@
         ship(1, i, *second_date(i))
         return carry
 
-    lax.fori_loop(1, n, second_step, 0)
+    lax.fori_loop(1, n, second_step, 0, unroll=n <= 4)
     keep(*second_date(0))
 
     early[s] = combine(1, e2_ref)

time: 38.2 us -> 38.1 us (level)
  no operation moved by 1% of the time
where the time goes in v4:
time: 38.1 us; the launch traced here: 37.8 us
  Pallas kernels  32.9 us (86%)
  local copies, waits for them, and re-layouts  3.03 us (8%)
  other arithmetic  1.2 us (3%)
  between operations  0.66 us (2%)
    pallas_call x1, Pallas kernels, per_device(): call(states_mid, states_late, offset_late.astype(f32).reshape(1, cols), v...  32.9 us
    unnamed x8, local copies, waits for them, and re-layouts  3.03 us

profile of v4, /device:TPU:0, one launch (start us, length us, event | category | flops | bytes accessed | tf_op | source)
XLA Modules:
  0.0 37.8 jit_solution(3978588372006086068)
XLA Ops:
  0.6 0.0 copy-start.1
  0.6 0.7 %copy-done.1 = bf16[2048]{0:T(1024)(128)(2,1)S(1)} copy-done((bf16[2048]{0:T(1024)(128)(2,1)S(1)}, bf16[2048]{0:T(1024)(128)(2,1)}, u32[]{:S(2)}) %copy-start.1) | copy-done | bytes 4120
  1.3 0.0 copy-start.2
  1.3 0.6 %reshape.18 = f32[2048]{0:T(1024)} convert(bf16[2048]{0:T(1024)(128)(2,1)S(1)} %copy-done.1) | non-fusion elementwise | flops 2048 | bytes 12288 | tf_op jit(solution)/shard_map/reshape | solution.py:411
  1.9 0.1 copy-done.2
  2.0 0.6 %reshape.20 = f32[2048]{0:T(1024)} convert(bf16[2048]{0:T(1024)(128)(2,1)S(1)} %copy-done.2) | non-fusion elementwise | flops 2048 | bytes 12288 | tf_op jit(solution)/shard_map/reshape | solution.py:413
  2.6 32.9 %shard_map.113 = (bf16[64,1024]{1,0:T(8,128)(2,1)}, bf16[64,1024]{1,0:T(8,128)(2,1)}) custom-call(bf16[1024,128]{1,0:T(8,128)(2,1)} %x1_hbm.1, bf16[2048,128]{1,0:T(8,128)(2,1)} %y1_hbm.1, f32[1,2048]{1,0:T(1,128)} %bitcast.9, bf16[64,2048]{1,0:T(8,128)(2,1)} %bitcast.11, f32[1,2048]{1,0:T(1,128)} %bitcast.10, bf16[64,1024]{1,0:T(8,128)(2,1)} %bitcast.12, ...), custom_call_target="tpu_custom_call" | custom-call | flops 1610612736 | bytes 4194304 | tf_op jit(solution)/shard_map/pallas_call | solution.py:408
  35.5 0.0 copy-start
  35.5 1.6 %copy.14 = bf16[1024,64]{0,1:T(8,128)(2,1)} copy(bf16[1024,64]{0,1:T(8,128)(2,1)} %bitcast.8) | data formatting | bytes 262144
  37.1 0.0 copy-done
  37.1 0.7 %copy.15 = bf16[1024,64]{0,1:T(8,128)(2,1)} copy(bf16[1024,64]{0,1:T(8,128)(2,1)S(1)} %bitcast.7) | data formatting | bytes 262144
Async XLA Ops:
  0.6 0.7 %copy-start.1 = (bf16[2048]{0:T(1024)(128)(2,1)S(1)}, bf16[2048]{0:T(1024)(128)(2,1)}, u32[]{:S(2)}) copy-start(bf16[2048]{0:T(1024)(128)(2,1)} %param.11) | copy-start | bytes 12292
  1.3 0.7 %copy-start.2 = (bf16[2048]{0:T(1024)(128)(2,1)S(1)}, bf16[2048]{0:T(1024)(128)(2,1)}, u32[]{:S(2)}) copy-start(bf16[2048]{0:T(1024)(128)(2,1)} %param.14) | copy-start | bytes 12292
  35.5 1.6 %copy-start = (bf16[64,1024]{1,0:T(8,128)(2,1)S(1)}, bf16[64,1024]{1,0:T(8,128)(2,1)}, u32[]{:S(2)}) copy-start(bf16[64,1024]{1,0:T(8,128)(2,1)} %get-tuple-element.5) | copy-start | bytes 393220
